TPU v7x, 32 devices: a whole 2x2x4 slice. The times are simulated.
32 devices in a mesh: pool: 4 (over y, core), col: 8 (over z, x).
Axes of the slice: x: 2, y: 2, z: 4, core: 2. Of those that a mesh axis runs over, the one named last changes fastest.
Arguments:
- pair_matrix: bfloat16 [1024, 12288], P('pool', 'col'), may hold values from -1.1953125 to 1.1953125
- band_energy: float32 [4, 4, 4096], P('pool'), may hold values from -2 to 2
- occupation: int32 [4, 4, 4096], P('pool'), may hold values 0 or 1
- pair_first: int32 [4, 256], P('pool'), may hold values from 0 to 4095
- pair_second: int32 [4, 256], P('pool'), may hold values from 0 to 4095
- pair_kpoint: int32 [4, 256], P('pool'), may hold values from 0 to 3
Outputs:
- chi_zero: float32 [12288, 12288], P('pool', 'col')
All inputs are finite; a program needn't handle non-finite values. No bound on the sum of `occupation` on one device may be relied on, other than what follows from the above.
Results may differ from a plain program's by a relative error of at most 0.012.
Values may be sent and summed in bfloat16 or wider, within the bound.
A program may use at most 64 MiB of HBM per device.

v0:
```python
import jax
import jax.numpy as jnp
from jax import lax
from jax.sharding import PartitionSpec as P


def broadcast(value, axis, source):
    kept = jnp.where(lax.axis_index(axis) == source, value, 0).astype(value.dtype)
    return lax.psum(kept, axis)


def pool_weight(energy, occupied, first, second, kpoint):
    bands = energy.shape[-1]
    flat_energy = energy.reshape(-1)
    flat_occupied = occupied.reshape(-1).astype(jnp.float32)
    index_first = kpoint * bands + first
    index_second = kpoint * bands + second
    gap = jnp.abs(jnp.take(flat_energy, index_second) - jnp.take(flat_energy, index_first))
    filled = jnp.take(flat_occupied, index_first) - jnp.take(flat_occupied, index_second)
    return 2.0 * filled / (1.0 + gap)


def per_device(pair_matrix, band_energy, occupation, pair_first, pair_second, pair_kpoint):
    weight = pool_weight(
        band_energy[0], occupation[0], pair_first[0], pair_second[0], pair_kpoint[0]
    )
    scaled = (pair_matrix.astype(jnp.float32) * weight[:, None]).astype(jnp.bfloat16)
    pools = lax.axis_size("pool")
    group = lax.axis_size("col") // pools
    width = pair_matrix.shape[1]
    pairs = pair_matrix.shape[0]
    all_pairs, all_scaled = (
        lax.all_gather(pair_matrix, "pool", axis=0, tiled=True),
        lax.all_gather(scaled, "pool", axis=0, tiled=True),
    )
    scaled_pools = all_scaled.reshape(pools, pairs, width)
    first_root = lax.axis_index("pool") * group

    def one_panel(step, total):
        panel = broadcast(all_pairs, "col", first_root + step)
        panel_pools = panel.reshape(pools, pairs, width)
        parts = lax.dot_general(
            panel_pools,
            scaled_pools,
            (((1,), (1,)), ((0,), (0,))),
            preferred_element_type=jnp.float32,
        )
        block = jnp.sum(parts.astype(jnp.bfloat16).astype(jnp.float32), axis=0)
        return lax.dynamic_update_slice_in_dim(total, block, step * width, 0)

    start_total = jnp.zeros((group * width, width), jnp.float32)
    chi_zero = lax.fori_loop(0, group, one_panel, start_total)
    return chi_zero


def solution(mesh):
    return jax.shard_map(
        per_device,
        mesh=mesh,
        in_specs=(
            P("pool", "col"),
            P("pool", None, None),
            P("pool", None, None),
            P("pool", None),
            P("pool", None),
            P("pool", None),
        ),
        out_specs=P("pool", "col"),
        check_vma=False,
    )
```

profile of v0, /device:TPU:5, one launch (start us, length us, event | category | flops | bytes accessed | tf_op | source)
XLA Modules:
  0.0 376.1 jit_solution(926134473882317400)
XLA Ops:
  6.5 0.0 copy-start
  6.5 0.0 all-gather.3.cloned.1.call-start
  6.5 0.7 all-gather.3.cloned.1.call-update
  7.3 0.0 all-gather.5.cloned.1.call-start
  7.3 0.8 copy.9
  8.2 0.7 multiply_add_fusion
  8.9 1.7 gather_fusion.3
  10.6 1.7 gather_fusion.2
  12.4 0.9 convert_bitcast_fusion
  13.2 1.7 gather_fusion.1
  15.0 1.7 gather_fusion
  16.7 0.0 copy-done
  16.7 1.1 multiply_convert_fusion
  17.8 0.0 all-gather.5.cloned.1.call-update
  17.8 20.1 %all-gather.3.cloned.1.call-done = bf16[1024,1536]{1,0:T(8,128)(2,1)} async-done(((bf16[256,1536]{1,0:T(8,128)(2,1)}), bf16[1024,1536]{1,0:T(8,128)(2,1)}) %all-gather.3.cloned.1.call-update) | async-done | bytes 3145744 | tf_op jit(solution)/shard_map/all_gather | solution.py:33
  37.9 30.1 %all-gather.5.cloned.1.call-done = bf16[1024,1536]{1,0:T(8,128)(2,1)} async-done(((bf16[256,1536]{1,0:T(8,128)(2,1)}), bf16[1024,1536]{1,0:T(8,128)(2,1)}) %all-gather.5.cloned.1.call-update) | async-done | bytes 3145744 | tf_op jit(solution)/shard_map/all_gather | solution.py:34
  68.1 9.3 %broadcast_in_dim.21 = f32[3072,1536]{1,0:T(8,128)} broadcast(f32[]{:T(128)} %constant.87.clone.1), dimensions={} | broadcast | bytes 18874372 | tf_op jit(solution)/shard_map/broadcast_in_dim | solution.py:51
  77.3 292.2 %while.15 = (s32[]{:T(128)}, f32[3072,1536]{1,0:T(8,128)}, s32[]{:T(128)}, bf16[1024,1536]{1,0:T(8,128)(2,1)}, bf16[4,256,1536]{2,1,0:T(8,128)(2,1)}, /*index=5*...) while((s32[]{:T(128)}, f32[3072,1536]{1,0:T(8,128)}, s32[]{:T(128)}, bf16[1024,1536]{1,0:T(8,128)(2,1)}, ...), condition=%wide.region_3.5_spmd, body=%wide.region_0.4_spmd.sunk | while | flops 4860936192 | bytes 78643464 | solution.py:52
  77.3 0.0 all-reduce.2.cloned.1.call-start
  77.3 0.2 broadcast_select_fusion.2
  77.5 2.8 copy.11
  80.4 0.0 copy-start.1
  80.4 0.0 all-reduce.2.cloned.1.call-update
  80.4 130.9 %all-reduce.2.cloned.1.call-done = bf16[4,256,1536]{1,2,0:T(8,128)(2,1)} async-done(((bf16[4,256,1536]{1,2,0:T(8,128)(2,1)}), bf16[4,256,1536]{1,2,0:T(8,128)(2,1)}) %all-reduce.2.cloned.1.call-update) | async-done | bytes 3145744 | tf_op jit(solution)/shard_map/while/body/eval_jaxpr/psum | solution.py:9
  211.3 0.0 copy-done.1
  211.3 8.1 %convert_reduce_fusion.2 = f32[1536,1536]{1,0:T(8,128)S(1)} fusion(bf16[4,256,1536]{1,2,0:T(8,128)(2,1)} %all-reduce.2.cloned.1.call-done, bf16[4,256,1536]{2,1,0:T(8,128)(2,1)S(1)} %copy-done.1), kind=kOutput, calls=%fused_computation.4.clone.1 | convolution fusion | flops 4857790464 | bytes 15728640 | tf_op jit(solution)/shard_map/while/body/eval_jaxpr/dot_general | solution.py:42
  219.5 4.6 %constant_dynamic-update-slice_fusion.2 = f32[3072,1536]{1,0:T(8,128)} fusion(f32[3072,1536]{1,0:T(8,128)} %get-tuple-element.193, f32[1536,1536]{1,0:T(8,128)S(1)} %convert_reduce_fusion.2, s32[]{:T(128)S(6)} %select_n.80), kind=kLoop, calls=%fused_computation.7.clone.1 | loop fusion | bytes 18874372 | tf_op jit(solution)/shard_map/while/body/eval_jaxpr/dynamic_update_slice | solution.py:49
  224.1 0.0 all-reduce.2.cloned.1.call-start
  224.1 0.2 broadcast_select_fusion.2
  224.3 2.8 copy.11
  227.1 0.0 copy-start.1
  227.1 0.0 all-reduce.2.cloned.1.call-update
  227.1 129.7 %all-reduce.2.cloned.1.call-done = bf16[4,256,1536]{1,2,0:T(8,128)(2,1)} async-done(((bf16[4,256,1536]{1,2,0:T(8,128)(2,1)}), bf16[4,256,1536]{1,2,0:T(8,128)(2,1)}) %all-reduce.2.cloned.1.call-update) | async-done | bytes 3145744 | tf_op jit(solution)/shard_map/while/body/eval_jaxpr/psum | solution.py:9
  356.8 0.0 copy-done.1
  356.8 8.1 %convert_reduce_fusion.2 = f32[1536,1536]{1,0:T(8,128)S(1)} fusion(bf16[4,256,1536]{1,2,0:T(8,128)(2,1)} %all-reduce.2.cloned.1.call-done, bf16[4,256,1536]{2,1,0:T(8,128)(2,1)S(1)} %copy-done.1), kind=kOutput, calls=%fused_computation.4.clone.1 | convolution fusion | flops 4857790464 | bytes 15728640 | tf_op jit(solution)/shard_map/while/body/eval_jaxpr/dot_general | solution.py:42
  364.9 4.6 %constant_dynamic-update-slice_fusion.2 = f32[3072,1536]{1,0:T(8,128)} fusion(f32[3072,1536]{1,0:T(8,128)} %get-tuple-element.193, f32[1536,1536]{1,0:T(8,128)S(1)} %convert_reduce_fusion.2, s32[]{:T(128)S(6)} %select_n.80), kind=kLoop, calls=%fused_computation.7.clone.1 | loop fusion | bytes 18874372 | tf_op jit(solution)/shard_map/while/body/eval_jaxpr/dynamic_update_slice | solution.py:49
  (6 shorter events, 0.0 us)
Async XLA Ops:
  6.5 10.2 %copy-start = (bf16[256,1536]{1,0:T(8,128)(2,1)S(1)}, bf16[256,1536]{1,0:T(8,128)(2,1)}, u32[]{:S(2)}) copy-start(bf16[256,1536]{1,0:T(8,128)(2,1)} %param.10) | copy-start | bytes 2359300
  6.5 31.4 %all-gather.3.cloned.1.call-start = ((), (), s32[]{:S(2)}) async-start(), calls=%async_computation | async-start | bytes 3932160 | tf_op jit(solution)/shard_map/all_gather | solution.py:33
  7.3 60.8 %all-gather.5.cloned.1.call-start = ((), (), s32[]{:S(2)}) async-start(), calls=%async_computation.1 | async-start | bytes 3932160 | tf_op jit(solution)/shard_map/all_gather | solution.py:34
  77.3 134.0 %all-reduce.2.cloned.1.call-start = ((), (), s32[]{:S(2)}) async-start(), calls=%async_computation.2 | async-start | bytes 6291456 | tf_op jit(solution)/shard_map/while/body/eval_jaxpr/psum | solution.py:9
  80.4 131.0 %copy-start.1 = (bf16[4,256,1536]{2,1,0:T(8,128)(2,1)S(1)}, bf16[4,256,1536]{2,1,0:T(8,128)(2,1)}, u32[]{:S(2)}) copy-start(bf16[4,256,1536]{2,1,0:T(8,128)(2,1)} %get-tuple-element.206) | copy-start | bytes 9437188 | tf_op jit(solution)/shard_map/while
  224.1 132.8 %all-reduce.2.cloned.1.call-start = ((), (), s32[]{:S(2)}) async-start(), calls=%async_computation.2 | async-start | bytes 6291456 | tf_op jit(solution)/shard_map/while/body/eval_jaxpr/psum | solution.py:9
  227.1 129.7 %copy-start.1 = (bf16[4,256,1536]{2,1,0:T(8,128)(2,1)S(1)}, bf16[4,256,1536]{2,1,0:T(8,128)(2,1)}, u32[]{:S(2)}) copy-start(bf16[4,256,1536]{2,1,0:T(8,128)(2,1)} %get-tuple-element.206) | copy-start | bytes 9437188 | tf_op jit(solution)/shard_map/while
Sparse Core Ops, SparseCore 0:
  8.9 28.9 all-gather.2
  39.5 28.5 all-gather.4
  81.7 129.5 all-reduce.1
  228.1 128.6 all-reduce.1
where the time goes:
time: 378 us; the launch traced here: 376 us
  waiting for transfers between devices  312 us (83%)
  local copies, waits for them, and re-layouts  31.9 us (8%)
  matrix products  16.2 us (4%)
  between operations  13.2 us (3%)
    psum x2, waiting for transfers between devices, broadcast(): return lax.psum(kept, axis)  261 us
    all_gather x1, waiting for transfers between devices, per_device(): lax.all_gather(scaled, 'pool', axis=0, tiled=True)  30.1 us
    all_gather x1, waiting for transfers between devices, per_device(): lax.all_gather(pair_matrix, 'pool', axis=0, tiled=True)  20.1 us
    dot_general x2, matrix products, one_panel(): lax.dot_general(panel_pools, scaled_pools, (((1,), (1,)), ((0,), (0,))),...  16.2 us
    broadcast_in_dim x1, local copies, waits for them, and re-layouts, per_device(): start_total = jnp.zeros((group * width, width), jnp.float32)  9.26 us
    dynamic_update_slice x2, local copies, waits for them, and re-layouts, one_panel(): return lax.dynamic_update_slice_in_dim(total, block, step * width, 0)  9.19 us
  transfers between devices with their start and end apart: 4, of which 4 were waited for; matrix products, arithmetic and copies ran while one was open for 3% of the time, Pallas kernels for 0%

commit v1 on v0

v1 whole, which is shorter than its diff:
```python
import functools

import jax
import jax.numpy as jnp
from jax import lax
from jax.experimental import pallas as pl
from jax.experimental.pallas import tpu as pltpu
from jax.sharding import PartitionSpec as P

MESH = pl.DeviceIdType.MESH
LANES = 128
PIECES = 4


def broadcast(value, axis, source):
    kept = jnp.where(lax.axis_index(axis) == source, value, 0).astype(value.dtype)
    return lax.psum(kept, axis)


def pool_weight(energy, occupied, first, second, kpoint):
    bands = energy.shape[-1]
    flat_energy = energy.reshape(-1)
    flat_occupied = occupied.reshape(-1).astype(jnp.float32)
    index_first = kpoint * bands + first
    index_second = kpoint * bands + second
    gap = jnp.abs(jnp.take(flat_energy, index_second) - jnp.take(flat_energy, index_first))
    filled = jnp.take(flat_occupied, index_first) - jnp.take(flat_occupied, index_second)
    return 2.0 * filled / (1.0 + gap)


def per_device_any(pair_matrix, band_energy, occupation, pair_first, pair_second, pair_kpoint):
    weight = pool_weight(
        band_energy[0], occupation[0], pair_first[0], pair_second[0], pair_kpoint[0]
    )
    pools = lax.axis_size("pool")
    group = lax.axis_size("col") // pools
    width = pair_matrix.shape[1]
    all_pairs = lax.all_gather(pair_matrix, "pool", axis=0, tiled=True)
    all_weight = lax.all_gather(weight, "pool", axis=0, tiled=True)
    all_scaled = (all_pairs.astype(jnp.float32) * all_weight[:, None]).astype(jnp.bfloat16)
    first_root = lax.axis_index("pool") * group

    def one_panel(step, total):
        panel = broadcast(all_pairs, "col", first_root + step)
        block = lax.dot_general(
            panel, all_scaled, (((0,), (0,)), ((), ())), preferred_element_type=jnp.float32
        )
        return lax.dynamic_update_slice_in_dim(total, block, step * width, 0)

    start_total = jnp.zeros((group * width, width), jnp.float32)
    return lax.fori_loop(0, group, one_panel, start_total)


def lookup(table, high, low):
    n = high.shape[1]
    rows = lax.broadcasted_iota(jnp.int32, (table.shape[0], n), 0)
    chosen = (rows == high).astype(jnp.float32)
    lines = lax.dot_general(
        table,
        chosen,
        (((0,), (0,)), ((), ())),
        precision=lax.Precision.HIGHEST,
        preferred_element_type=jnp.float32,
    )
    lanes = lax.broadcasted_iota(jnp.int32, (table.shape[1], n), 0)
    return jnp.sum(jnp.where(lanes == low, lines, 0.0), axis=0, keepdims=True)


def gather_kernel(
    depth, m_ref, energy_ref, occupied_ref, first_ref, second_ref, kpoint_ref,
    rows_ref, cols_ref, relay_ref, weight_ref,
    energy_table, occupied_table, own_weight,
    own_sem, line_in, relay_in, cross_in, side_in, mate_in, over_in, back_in, w_in,
    line_up, line_down, line_side, relay_up, relay_down, relay_over, cross_side,
    mate_out, over_out, back_out, w_out,
):
    pairs, width = m_ref.shape
    q, c = lax.axis_index("pool"), lax.axis_index("col")
    y, core = q // 2, q % 2
    z, x = c // 2, c % 2
    dest_z, relay_z = q, (q + 2) % 4
    mate = y * 2 + (1 - core)
    over = (1 - y) * 2 + core
    diagonal = (1 - y) * 2 + (1 - core)
    side = z * 2 + (1 - x)
    piece = pairs // PIECES
    count = 2 * PIECES
    half = 2 * pairs

    has_up, has_down = z < depth - 1, z > 0
    at_source, at_relay = z == dest_z, z == relay_z

    barrier = pltpu.get_barrier_semaphore()

    def greet(pool, col):
        pl.semaphore_signal(barrier, inc=1, device_id=(pool, col), device_id_type=MESH)

    greet(mate, c)
    greet(over, c)
    greet(diagonal, c)
    greet(q, side)

    @pl.when(has_up)
    def _():
        greet(q, c + 2)

    @pl.when(has_down)
    def _():
        greet(q, c - 2)

    neighbours = 4 + has_up.astype(jnp.int32) + has_down.astype(jnp.int32)
    pl.semaphore_wait(barrier, neighbours)

    def remote(source, target, send, receive, pool, col):
        return pltpu.make_async_remote_copy(
            src_ref=source, dst_ref=target, send_sem=send, recv_sem=receive,
            device_id=(pool, col), device_id_type=MESH,
        )

    def spot(n):
        return lax.rem(core * PIECES + n, count)

    def col_at(pool, n):
        return cols_ref.at[pl.ds(pl.multiple_of(pool * pairs + n * piece, piece), piece)]

    def row_at(which_x, which_y, n):
        start = pl.multiple_of(which_y * half + spot(n) * piece, piece)
        return rows_ref.at[which_x, pl.ds(start, piece)]

    def relay_at(n):
        return relay_ref.at[pl.ds(pl.multiple_of(spot(n) * piece, piece), piece)]

    def own_at(n):
        return m_ref.at[pl.ds(pl.multiple_of(n * piece, piece), piece)]

    def to_mate(n):
        return remote(own_at(n), col_at(q, n), mate_out.at[n], mate_in.at[n], mate, c)

    def from_mate(n):
        return remote(own_at(n), col_at(mate, n), mate_out.at[n], mate_in.at[n], mate, c)

    def to_over(n):
        return remote(own_at(n), col_at(q, n), over_out.at[n], over_in.at[n], over, c)

    def from_over(n):
        return remote(own_at(n), col_at(over, n), over_out.at[n], over_in.at[n], over, c)

    def to_back(n):
        ref = col_at(over, n)
        return remote(ref, ref, back_out.at[n], back_in.at[n], mate, c)

    def from_back(n):
        ref = col_at(diagonal, n)
        return remote(ref, ref, back_out.at[n], back_in.at[n], mate, c)

    def line(n, step, send):
        ref = row_at(x, y, n)
        return remote(ref, ref, send.at[n], line_in.at[n], q, c + step)

    def relay(n, step, send):
        ref = relay_at(n)
        return remote(ref, ref, send.at[n], relay_in.at[n], q, c + step)

    def relay_cross(n):
        return remote(
            relay_at(n), row_at(x, y, n), relay_over.at[n], cross_in.at[n], over, c
        )

    def line_to_side(n):
        ref = row_at(x, y, n)
        return remote(ref, ref, line_side.at[n], side_in.at[0, n], q, side)

    def cross_to_side(n):
        ref = row_at(x, 1 - y, n)
        return remote(ref, ref, cross_side.at[n], side_in.at[1, n], q, side)

    line_goes_up = has_up & (z >= dest_z)
    line_goes_down = has_down & (z <= dest_z)
    relay_goes_up = has_up & (z >= relay_z)
    relay_goes_down = has_down & (z <= relay_z)

    def line_step(n):
        pltpu.make_async_copy(row_at(x, y, n), row_at(x, y, n), line_in.at[n]).wait()

        @pl.when(line_goes_up)
        def _():
            line(n, 2, line_up).start()

        @pl.when(line_goes_down)
        def _():
            line(n, -2, line_down).start()

        line_to_side(n).start()

    def relay_step(n):
        pltpu.make_async_copy(relay_at(n), relay_at(n), relay_in.at[n]).wait()

        @pl.when(relay_goes_up)
        def _():
            relay(n, 2, relay_up).start()

        @pl.when(relay_goes_down)
        def _():
            relay(n, -2, relay_down).start()

        relay_cross(n).start()

    def cross_step(n):
        ref = row_at(x, 1 - y, n)
        pltpu.make_async_copy(ref, ref, cross_in.at[n]).wait()
        cross_to_side(n).start()

    def loop(times, body):
        def one(n, carry):
            body(n)
            return carry

        lax.fori_loop(0, times, one, 0)

    def begin(n):
        to_mate(n).start()
        pltpu.make_async_copy(own_at(n), col_at(q, n), own_sem.at[n]).start()

        @pl.when(at_source)
        def _():
            pltpu.make_async_copy(own_at(n), row_at(x, y, n), line_in.at[n]).start()

        @pl.when(at_relay)
        def _():
            pltpu.make_async_copy(own_at(n), relay_at(n), relay_in.at[n]).start()

    loop(PIECES, begin)

    def begin_mate(n):
        from_mate(n).wait_recv()

        @pl.when(at_source)
        def _():
            pltpu.make_async_copy(
                col_at(mate, n), row_at(x, y, PIECES + n), line_in.at[PIECES + n]
            ).start()

        @pl.when(at_relay)
        def _():
            pltpu.make_async_copy(
                col_at(mate, n), relay_at(PIECES + n), relay_in.at[PIECES + n]
            ).start()

    @pl.when(at_source)
    def _():
        loop(PIECES, line_step)

    @pl.when(at_relay)
    def _():
        loop(PIECES, relay_step)

    loop(PIECES, begin_mate)

    @pl.when(at_source)
    def _():
        loop(PIECES, lambda n: line_step(PIECES + n))

    @pl.when(at_relay)
    def _():
        loop(PIECES, lambda n: relay_step(PIECES + n))

    loop(PIECES, lambda n: to_over(n).start())

    kpoints, bands = energy_ref.shape[1:]
    for block in range(bands // LANES):
        here = slice(block * LANES, (block + 1) * LANES)
        there = slice(block * kpoints, (block + 1) * kpoints)
        energy_table[there, :] = energy_ref[0, :, here]
        occupied_table[there, :] = occupied_ref[0, :, here].astype(jnp.float32)

    def values(band):
        high = lax.shift_right_logical(band, 7) * kpoints + kpoint_ref[...]
        low = lax.bitwise_and(band, LANES - 1)
        return (
            lookup(energy_table[...], high, low),
            lookup(occupied_table[...], high, low),
        )

    energy_first, filled_first = values(first_ref[...])
    energy_second, filled_second = values(second_ref[...])
    gap = jnp.abs(energy_second - energy_first)
    weight = 2.0 * (filled_first - filled_second) / (1.0 + gap)
    own_weight[...] = jnp.broadcast_to(weight, own_weight.shape)

    others = (mate, over, diagonal)

    def send_weight(n):
        return remote(
            own_weight, weight_ref.at[q], w_out.at[n], w_in.at[n], others[n], c
        )

    keep_weight = pltpu.make_async_copy(own_weight, weight_ref.at[q], own_sem.at[PIECES])
    keep_weight.start()
    for n in range(3):
        send_weight(n).start()

    def through(n):
        @pl.when(jnp.logical_not(at_relay))
        def _():
            relay_step(n)

        @pl.when(jnp.logical_not(at_source))
        def _():
            line_step(n)

        @pl.when(n > 0)
        def _():
            cross_step(n - 1)

    loop(count, through)
    cross_step(count - 1)

    def give_back(n):
        from_over(n).wait_recv()
        to_back(n).start()

    loop(PIECES, give_back)

    def finish(n):
        pltpu.make_async_copy(
            row_at(1 - x, y, n), row_at(1 - x, y, n), side_in.at[0, n]
        ).wait()
        pltpu.make_async_copy(
            row_at(1 - x, 1 - y, n), row_at(1 - x, 1 - y, n), side_in.at[1, n]
        ).wait()

        @pl.when(line_goes_up)
        def _():
            line(n, 2, line_up).wait_send()

        @pl.when(line_goes_down)
        def _():
            line(n, -2, line_down).wait_send()

        @pl.when(relay_goes_up)
        def _():
            relay(n, 2, relay_up).wait_send()

        @pl.when(relay_goes_down)
        def _():
            relay(n, -2, relay_down).wait_send()

        line_to_side(n).wait_send()
        relay_cross(n).wait_send()
        cross_to_side(n).wait_send()

    loop(count, finish)

    def finish_cols(n):
        from_back(n).wait_recv()
        to_mate(n).wait_send()
        to_over(n).wait_send()
        to_back(n).wait_send()
        pltpu.make_async_copy(own_at(n), col_at(q, n), own_sem.at[n]).wait()

    loop(PIECES, finish_cols)
    keep_weight.wait()
    for n in range(3):
        send_weight(n).wait()


def gather(pair_matrix, band_energy, occupation, pair_first, pair_second, pair_kpoint, depth):
    pairs, width = pair_matrix.shape
    kpoints, bands = band_energy.shape[1:]
    lines = kpoints * bands // LANES
    count = 2 * PIECES
    pools = lax.axis_size("pool")
    dma = pltpu.SemaphoreType.DMA
    anywhere = pl.BlockSpec(memory_space=pl.ANY)
    vmem = pl.BlockSpec(memory_space=pltpu.VMEM)
    return pl.pallas_call(
        functools.partial(gather_kernel, depth),
        out_shape=(
            jax.ShapeDtypeStruct((2, pools * pairs, width), jnp.bfloat16),
            jax.ShapeDtypeStruct((pools * pairs, width), jnp.bfloat16),
            jax.ShapeDtypeStruct((2 * pairs, width), jnp.bfloat16),
            jax.ShapeDtypeStruct((pools, 8, pairs), jnp.float32),
        ),
        in_specs=[anywhere] + [vmem] * 5,
        out_specs=(anywhere,) * 4,
        scratch_shapes=[
            pltpu.VMEM((lines, LANES), jnp.float32),
            pltpu.VMEM((lines, LANES), jnp.float32),
            pltpu.VMEM((8, pairs), jnp.float32),
            dma((PIECES + 1,)),
            dma((count,)), dma((count,)), dma((count,)), dma((2, count)),
            dma((PIECES,)), dma((PIECES,)), dma((PIECES,)), dma((3,)),
            dma((count,)), dma((count,)), dma((count,)),
            dma((count,)), dma((count,)), dma((count,)), dma((count,)),
            dma((PIECES,)), dma((PIECES,)), dma((PIECES,)), dma((3,)),
        ],
        compiler_params=pltpu.CompilerParams(collective_id=0, has_side_effects=True),
    )(pair_matrix, band_energy, occupation, pair_first, pair_second, pair_kpoint)


def multiply_kernel(rows_ref, cols_ref, weight_ref, out_ref, scaled):
    @pl.when((pl.program_id(0) == 0) & (pl.program_id(1) == 0))
    def _():
        pools, _, pairs = weight_ref.shape
        for pool in range(pools):
            here = pl.ds(pool * pairs, pairs)
            column = jnp.transpose(weight_ref[pool])[:, :1]
            scaled[here, :] = (cols_ref[here, :].astype(jnp.float32) * column).astype(jnp.bfloat16)

    out_ref[...] = lax.dot_general(
        rows_ref[0], scaled[...], (((0,), (0,)), ((), ())), preferred_element_type=jnp.float32
    )


def multiply(rows, cols, weight):
    halves, pairs, width = rows.shape
    tile = width // 6
    tiles = width // tile
    return pl.pallas_call(
        multiply_kernel,
        grid=(halves, tiles),
        out_shape=jax.ShapeDtypeStruct((halves * width, width), jnp.float32),
        in_specs=[
            pl.BlockSpec((1, pairs, tile), lambda h, t: (h, 0, t)),
            pl.BlockSpec((pairs, width), lambda h, t: (0, 0)),
            pl.BlockSpec(weight.shape, lambda h, t: (0, 0, 0)),
        ],
        out_specs=pl.BlockSpec((tile, width), lambda h, t: (h * tiles + t, 0)),
        scratch_shapes=[pltpu.VMEM((pairs, width), jnp.bfloat16)],
        compiler_params=pltpu.CompilerParams(vmem_limit_bytes=40 * 1024 * 1024),
    )(rows, cols, weight)


def per_device(pair_matrix, band_energy, occupation, pair_first, pair_second, pair_kpoint):
    pools, cols = lax.axis_size("pool"), lax.axis_size("col")
    if pools != 4 or cols != 2 * pools or pair_matrix.shape[1] % (6 * LANES):
        return per_device_any(
            pair_matrix, band_energy, occupation, pair_first, pair_second, pair_kpoint
        )
    rows, columns, _, weight = gather(
        pair_matrix, band_energy, occupation, pair_first, pair_second, pair_kpoint, cols // 2
    )
    return multiply(rows, columns, weight)


def solution(mesh):
    return jax.shard_map(
        per_device,
        mesh=mesh,
        in_specs=(
            P("pool", "col"),
            P("pool", None, None),
            P("pool", None, None),
            P("pool", None),
            P("pool", None),
            P("pool", None),
        ),
        out_specs=P("pool", "col"),
        check_vma=False,
    )
```

time: 378 us -> 175 us (0.46)
  waiting for transfers between devices: 312 us -> 0 us
  Pallas kernels: 0 us -> 169 us
  local copies, waits for them, and re-layouts: 31.9 us -> 5.42 us
  matrix products: 16.2 us -> 0 us
  between operations: 13.2 us -> 0.02 us
    psum x2 -> x0, waiting for transfers between devices: 261 us -> none  [broadcast(): return lax.psum(kept, axis)]
    pallas_call x0 -> x2, Pallas kernels: none -> 169 us  [the longest x1 154 us: gather(): pl.pallas_call(functools.partial(gather_kernel, depth), out_shape=(jax.Sh...]
    all_gather x2 -> x0, waiting for transfers between devices: 50.2 us -> none  [the longest x1 30.1 us: per_device(): lax.all_gather(scaled, 'pool', axis=0, tiled=True)]
    dot_general x2 -> x0, matrix products: 16.2 us -> none  [one_panel(): lax.dot_general(panel_pools, scaled_pools, (((1,), (1,)), ((0,), (0,))),...]
    broadcast_in_dim x1 -> x0, local copies, waits for them, and re-layouts: 9.26 us -> none  [per_device(): start_total = jnp.zeros((group * width, width), jnp.float32)]
    dynamic_update_slice x2 -> x0, local copies, waits for them, and re-layouts: 9.19 us -> none  [one_panel(): return lax.dynamic_update_slice_in_dim(total, block, step * width, 0)]
    gather x4 -> x0, local copies, waits for them, and re-layouts: 6.89 us -> none  [the longest x1 1.72 us: pool_weight(): jnp.take(flat_occupied, index_second)]
    reshape x2 -> x0, local copies, waits for them, and re-layouts: 5.65 us -> none  [one_panel(): panel_pools = panel.reshape(pools, pairs, width)]
  transfers between devices with their start and end apart: 4 -> 0, of which waited for: 4 -> 0; matrix products, arithmetic and copies ran while one was open for 3% -> 0% of each run, Pallas kernels for 0% -> 0%
where the time goes in v1:
time: 175 us
  Pallas kernels  169 us (97%)
  local copies, waits for them, and re-layouts  5.42 us (3%)
    pallas_call x1, Pallas kernels, gather(): pl.pallas_call(functools.partial(gather_kernel, depth), out_shape=(jax.Sh...  154 us
    pallas_call x1, Pallas kernels, multiply(): pl.pallas_call(multiply_kernel, grid=(halves, tiles), out_shape=jax.Shape...  14.9 us
    unnamed x6, local copies, waits for them, and re-layouts  5.42 us

profile of v1, /device:TPU:5, one launch (start us, length us, event | category | flops | bytes accessed | tf_op | source)
XLA Modules:
  0.0 174.7 jit_solution(15483983047728014687)
XLA Ops:
  0.0 154.3 %shard_map.64 = (bf16[2,1024,1536]{2,1,0:T(8,128)(2,1)}, bf16[1024,1536]{1,0:T(8,128)(2,1)}, bf16[512,1536]{1,0:T(8,128)(2,1)}, f32[4,8,256]{2,1,0:T(8,128)}) custom-call(bf16[256,1536]{1,0:T(8,128)(2,1)} %m_ref.1, f32[1,4,4096]{2,1,0:T(4,128)} %energy_ref.1, s32[1,4,4096]{2,1,0:T(4,128)} %occupied_ref.1, s32[1,256]{1,0:T(1,128)} %first_ref.1, ...), custom_call_target="tpu_custom_call" | custom-call | tf_op jit(solution)/shard_map/pallas_call | solution.py:376
  154.4 0.0 copy-start
  154.4 2.8 %copy-done = bf16[2,1024,1536]{2,1,0:T(8,128)(2,1)S(1)} copy-done((bf16[2,1024,1536]{2,1,0:T(8,128)(2,1)S(1)}, bf16[2,1024,1536]{2,1,0:T(8,128)(2,1)}, u32[]{:S(2)}) %copy-start) | copy-done | bytes 6291480
  157.1 0.0 copy-start.1
  157.1 1.9 %copy-done.1 = bf16[1024,1536]{1,0:T(8,128)(2,1)S(1)} copy-done((bf16[1024,1536]{1,0:T(8,128)(2,1)S(1)}, bf16[1024,1536]{1,0:T(8,128)(2,1)}, u32[]{:S(2)}) %copy-start.1) | copy-done | bytes 3145752
  159.0 0.0 copy-start.2
  159.0 0.8 copy-done.2
  159.8 14.9 %shard_map.65 = f32[3072,1536]{1,0:T(8,128)} custom-call(bf16[2,1024,1536]{2,1,0:T(8,128)(2,1)S(1)} %copy-done, bf16[1024,1536]{1,0:T(8,128)(2,1)S(1)} %copy-done.1, f32[4,8,256]{2,1,0:T(8,128)S(1)} %copy-done.2), custom_call_target="tpu_custom_call" | custom-call | tf_op jit(solution)/shard_map/pallas_call | solution.py:419
Async XLA Ops:
  154.4 2.8 %copy-start = (bf16[2,1024,1536]{2,1,0:T(8,128)(2,1)S(1)}, bf16[2,1024,1536]{2,1,0:T(8,128)(2,1)}, u32[]{:S(2)}) copy-start(bf16[2,1024,1536]{2,1,0:T(8,128)(2,1)} %get-tuple-element.8.rows_ref) | copy-start | bytes 18874372
  157.1 1.9 %copy-start.1 = (bf16[1024,1536]{1,0:T(8,128)(2,1)S(1)}, bf16[1024,1536]{1,0:T(8,128)(2,1)}, u32[]{:S(2)}) copy-start(bf16[1024,1536]{1,0:T(8,128)(2,1)} %get-tuple-element.9.cols_ref) | copy-start | bytes 9437188
  159.0 0.8 copy-start.2

commit v2 on v1

--- a/solution.py
+++ b/solution.py
@@ -9,7 +9,10 @@
 
 MESH = pl.DeviceIdType.MESH
 LANES = 128
-PIECES = 4
+PIECES = 8
+HOP = 1
+CROSS = 2
+OVER = 4
 
 
 def broadcast(value, axis, source):
@@ -68,7 +71,7 @@
 
 def gather_kernel(
     depth, m_ref, energy_ref, occupied_ref, first_ref, second_ref, kpoint_ref,
-    rows_ref, cols_ref, relay_ref, weight_ref,
+    rows_ref, cols_ref, weight_ref, relay_ref,
     energy_table, occupied_table, own_weight,
     own_sem, line_in, relay_in, cross_in, side_in, mate_in, over_in, back_in, w_in,
     line_up, line_down, line_side, relay_up, relay_down, relay_over, cross_side,
@@ -264,7 +267,6 @@
     def _():
         loop(PIECES, lambda n: relay_step(PIECES + n))
 
-    loop(PIECES, lambda n: to_over(n).start())
 
     kpoints, bands = energy_ref.shape[1:]
     for block in range(bands // LANES):
@@ -299,21 +301,31 @@
     for n in range(3):
         send_weight(n).start()
 
-    def through(n):
-        @pl.when(jnp.logical_not(at_relay))
-        def _():
-            relay_step(n)
-
-        @pl.when(jnp.logical_not(at_source))
-        def _():
-            line_step(n)
-
-        @pl.when(n > 0)
-        def _():
-            cross_step(n - 1)
-
-    loop(count, through)
-    cross_step(count - 1)
+    line_late = HOP * jnp.abs(z - dest_z)
+    relay_late = HOP * jnp.abs(z - relay_z)
+    cross_late = line_late + CROSS
+
+    def through(t):
+        n_relay, n_line, n_cross = t - relay_late, t - line_late, t - cross_late
+        n_over = t - OVER
+
+        @pl.when((z != relay_z) & (n_relay >= 0) & (n_relay < count))
+        def _():
+            relay_step(n_relay)
+
+        @pl.when((z != dest_z) & (n_line >= 0) & (n_line < count))
+        def _():
+            line_step(n_line)
+
+        @pl.when((n_cross >= 0) & (n_cross < count))
+        def _():
+            cross_step(n_cross)
+
+        @pl.when((n_over >= 0) & (n_over < PIECES))
+        def _():
+            to_over(n_over).start()
+
+    loop(count + HOP * (depth - 1) + CROSS, through)
 
     def give_back(n):
         from_over(n).wait_recv()
@@ -371,19 +383,18 @@
     count = 2 * PIECES
     pools = lax.axis_size("pool")
     dma = pltpu.SemaphoreType.DMA
-    anywhere = pl.BlockSpec(memory_space=pl.ANY)
     vmem = pl.BlockSpec(memory_space=pltpu.VMEM)
     return pl.pallas_call(
         functools.partial(gather_kernel, depth),
         out_shape=(
             jax.ShapeDtypeStruct((2, pools * pairs, width), jnp.bfloat16),
             jax.ShapeDtypeStruct((pools * pairs, width), jnp.bfloat16),
-            jax.ShapeDtypeStruct((2 * pairs, width), jnp.bfloat16),
             jax.ShapeDtypeStruct((pools, 8, pairs), jnp.float32),
         ),
-        in_specs=[anywhere] + [vmem] * 5,
-        out_specs=(anywhere,) * 4,
+        in_specs=[vmem] * 6,
+        out_specs=(vmem,) * 3,
         scratch_shapes=[
+            pltpu.VMEM((2 * pairs, width), jnp.bfloat16),
             pltpu.VMEM((lines, LANES), jnp.float32),
             pltpu.VMEM((lines, LANES), jnp.float32),
             pltpu.VMEM((8, pairs), jnp.float32),
@@ -394,41 +405,10 @@
             dma((count,)), dma((count,)), dma((count,)), dma((count,)),
             dma((PIECES,)), dma((PIECES,)), dma((PIECES,)), dma((3,)),
         ],
-        compiler_params=pltpu.CompilerParams(collective_id=0, has_side_effects=True),
+        compiler_params=pltpu.CompilerParams(
+            collective_id=0, has_side_effects=True, vmem_limit_bytes=32 * 1024 * 1024
+        ),
     )(pair_matrix, band_energy, occupation, pair_first, pair_second, pair_kpoint)
-
-
-def multiply_kernel(rows_ref, cols_ref, weight_ref, out_ref, scaled):
-    @pl.when((pl.program_id(0) == 0) & (pl.program_id(1) == 0))
-    def _():
-        pools, _, pairs = weight_ref.shape
-        for pool in range(pools):
-            here = pl.ds(pool * pairs, pairs)
-            column = jnp.transpose(weight_ref[pool])[:, :1]
-            scaled[here, :] = (cols_ref[here, :].astype(jnp.float32) * column).astype(jnp.bfloat16)
-
-    out_ref[...] = lax.dot_general(
-        rows_ref[0], scaled[...], (((0,), (0,)), ((), ())), preferred_element_type=jnp.float32
-    )
-
-
-def multiply(rows, cols, weight):
-    halves, pairs, width = rows.shape
-    tile = width // 6
-    tiles = width // tile
-    return pl.pallas_call(
-        multiply_kernel,
-        grid=(halves, tiles),
-        out_shape=jax.ShapeDtypeStruct((halves * width, width), jnp.float32),
-        in_specs=[
-            pl.BlockSpec((1, pairs, tile), lambda h, t: (h, 0, t)),
-            pl.BlockSpec((pairs, width), lambda h, t: (0, 0)),
-            pl.BlockSpec(weight.shape, lambda h, t: (0, 0, 0)),
-        ],
-        out_specs=pl.BlockSpec((tile, width), lambda h, t: (h * tiles + t, 0)),
-        scratch_shapes=[pltpu.VMEM((pairs, width), jnp.bfloat16)],
-        compiler_params=pltpu.CompilerParams(vmem_limit_bytes=40 * 1024 * 1024),
-    )(rows, cols, weight)
 
 
 def per_device(pair_matrix, band_energy, occupation, pair_first, pair_second, pair_kpoint):
@@ -437,10 +417,16 @@
         return per_device_any(
             pair_matrix, band_energy, occupation, pair_first, pair_second, pair_kpoint
         )
-    rows, columns, _, weight = gather(
+    rows, columns, weight = gather(
         pair_matrix, band_energy, occupation, pair_first, pair_second, pair_kpoint, cols // 2
     )
-    return multiply(rows, columns, weight)
+    scaled = (
+        columns.astype(jnp.float32) * weight[:, 0, :].reshape(-1)[:, None]
+    ).astype(jnp.bfloat16)
+    product = lax.dot_general(
+        rows, scaled, (((1,), (0,)), ((), ())), preferred_element_type=jnp.float32
+    )
+    return product.reshape(-1, columns.shape[1])
 
 
 def solution(mesh):

time: 175 us -> 109 us (0.62)
  Pallas kernels: 169 us -> 89.6 us
  matrix products: 0 us -> 13.8 us
    pallas_call x1, Pallas kernels: 154 us -> 89.6 us  [gather(): pl.pallas_call(functools.partial(gather_kernel, depth), out_shape=(jax.Sh...]
    pallas_call x1 -> x0, Pallas kernels: 14.9 us -> none  [multiply(): pl.pallas_call(multiply_kernel, grid=(halves, tiles), out_shape=jax.Shape...]
    dot_general x0 -> x1, matrix products: none -> 13.8 us  [per_device(): lax.dot_general(rows, scaled, (((1,), (0,)), ((), ())), preferred_element...]
    unnamed x6 -> x12, local copies, waits for them, and re-layouts: 5.42 us -> 4.85 us
where the time goes in v2:
time: 109 us; the launch traced here: 108 us
  Pallas kernels  89.6 us (82%)
  matrix products  13.8 us (13%)
  local copies, waits for them, and re-layouts  4.85 us (4%)
    pallas_call x1, Pallas kernels, gather(): pl.pallas_call(functools.partial(gather_kernel, depth), out_shape=(jax.Sh...  89.6 us
    dot_general x1, matrix products, per_device(): lax.dot_general(rows, scaled, (((1,), (0,)), ((), ())), preferred_element...  13.8 us
    unnamed x12, local copies, waits for them, and re-layouts  4.85 us

profile of v2, /device:TPU:5, one launch (start us, length us, event | category | flops | bytes accessed | tf_op | source)
XLA Modules:
  0.0 108.3 jit_solution(11805168874841949076)
XLA Ops:
  0.0 0.0 copy-start
  0.0 1.1 %copy-done = bf16[256,1536]{1,0:T(8,128)(2,1)S(1)} copy-done((bf16[256,1536]{1,0:T(8,128)(2,1)S(1)}, bf16[256,1536]{1,0:T(8,128)(2,1)}, u32[]{:S(2)}) %copy-start) | copy-done | bytes 786456
  1.1 0.0 copy-start.1
  1.1 0.8 copy-done.1
  2.0 0.0 copy-start.2
  2.0 0.8 copy-done.2
  2.8 0.0 copy-start.3
  2.8 0.7 copy-done.3
  3.5 0.0 copy-start.4
  3.5 0.7 copy-done.4
  4.2 0.0 copy-start.5
  4.2 0.7 copy-done.5
  4.9 89.6 %shard_map.64 = (bf16[2,1024,1536]{2,1,0:T(8,128)(2,1)S(1)}, bf16[1024,1536]{1,0:T(8,128)(2,1)S(1)}, f32[4,8,256]{2,1,0:T(8,128)S(1)}) custom-call(bf16[256,1536]{1,0:T(8,128)(2,1)S(1)} %copy-done, f32[1,4,4096]{2,1,0:T(4,128)S(1)} %copy-done.1, s32[1,4,4096]{2,1,0:T(4,128)S(1)} %copy-done.2, s32[1,256]{1,0:T(1,128)S(1)} %copy-done.3, ...), custom_call_target="tpu_custom_call" | custom-call | tf_op jit(solution)/shard_map/pallas_call | solution.py:387
  94.4 13.8 %fusion.1 = f32[2,1536,1536]{2,1,0:T(8,128)} fusion(bf16[2,1024,1536]{2,1,0:T(8,128)(2,1)S(1)} %get-tuple-element.8, bf16[1024,1536]{1,0:T(8,128)(2,1)S(1)} %get-tuple-element.9, f32[1024]{0:T(1024)S(1)} %bitcast.6), kind=kOutput, calls=%fused_computation.2 | convolution fusion | flops 9668395008 | bytes 28315648 | tf_op jit(solution)/shard_map/dot_general | solution.py:426
  (1 shorter events, 0.0 us)
Async XLA Ops:
  0.0 1.1 %copy-start = (bf16[256,1536]{1,0:T(8,128)(2,1)S(1)}, bf16[256,1536]{1,0:T(8,128)(2,1)}, u32[]{:S(2)}) copy-start(bf16[256,1536]{1,0:T(8,128)(2,1)} %m_ref.1) | copy-start | bytes 2359300
  1.1 0.8 copy-start.1
  2.0 0.8 copy-start.2
  2.8 0.7 copy-start.3
  3.5 0.7 copy-start.4
  4.2 0.7 copy-start.5
